TPU v7x, 32 devices: a whole 2x2x4 slice. The times are simulated.
32 devices in a mesh: case: 2 (over x), space: 16 (over z, y, core).
Axes of the slice: x: 2, y: 2, z: 4, core: 2. Of those that a mesh axis runs over, the one named last changes fastest.
Arguments:
- snapshots: float32 [1024, 8192], P('space', 'case'), parts along dimension 1, may hold values from -6 to 6
- weights: float32 [8192], P(('case', 'space')), parts along dimension 0, may hold values from 0.25 to 4
- counts: int32 [32], P(('case', 'space')), parts along dimension 0, may hold values from 85 to 256, as said below
- starts: int32 [8], replicated, may hold values from 0 to 768, as said below
Outputs:
- modes: bfloat16 [2, 8, 129, 8192], P(None, None, None, ('case', 'space')), parts along dimension 3
- r_factor: float32 [2, 258, 8, 8], P(None, 'case'), parts along dimension 1
There are 2 independent parts, one for each index of `case`. A program takes and returns all parts, laid end to end along the dimension named above; an argument that names none is the same for every part. Nothing has to cross between parts.
Inputs may be any that keep to these rules, and one draw needn't show every extreme that they name: The first block starts at 0 and the last at 768. The live points of a shard are its first counts slots; some shard is full.
All inputs are finite; a program needn't handle non-finite values.
Results may differ from a plain program's by a relative error of at most 0.001.
Values sent between devices are 32-bit elements; how exact they have to be, the bound alone decides.
A program may use at most 256 MiB of HBM per device.

v0:
```python
import jax
import jax.numpy as jnp
from jax import lax
from jax.sharding import PartitionSpec as P

NFFT = 256
NBLK = 8


def combined_all(value, axis, join):
    pieces = jax.tree.map(lambda part: lax.all_gather(part, axis), value)
    head = jax.tree.map(lambda part: part[0], pieces)
    tail = jax.tree.map(lambda part: part[1:], pieces)
    running, _ = lax.scan(lambda running, piece: (join(running, piece), None), head, tail)
    return running


def window_table():
    moment = jnp.arange(NFFT, dtype=jnp.int32)
    harmonic = jnp.arange(NFFT // 2 + 1, dtype=jnp.int32)
    hann_window = 0.5 - 0.5 * jnp.cos(2.0 * jnp.pi * moment.astype(jnp.float32) / NFFT)
    norm_scale = 1.0 / jnp.sqrt(jnp.sum(hann_window * hann_window))
    folded = harmonic[:, None] * moment[None, :] % NFFT
    angle_table = 2.0 * jnp.pi * folded.astype(jnp.float32) / NFFT
    cosine = jnp.cos(angle_table) * (hann_window * norm_scale)[None, :]
    sine = -jnp.sin(angle_table) * (hann_window * norm_scale)[None, :]
    return jnp.concatenate([cosine, sine], axis=0)


def realize(record, starts, dft_table):
    centered = record - jnp.mean(record, axis=0, keepdims=True)
    outputs = []
    for block_id in range(NBLK):
        segment = lax.dynamic_slice_in_dim(centered, starts[block_id], NFFT, 0)
        outputs.append(
            jnp.dot(
                dft_table,
                segment,
                precision=lax.Precision.HIGHEST,
                preferred_element_type=jnp.float32,
            )
        )
    return jnp.stack(outputs, axis=0)


def gram_parts(realized, live_area):
    half_f = realized.shape[1] // 2
    real_part = realized[:, :half_f]
    imag_part = realized[:, half_f:]
    weighted_re = real_part * live_area
    weighted_im = imag_part * live_area
    high = lax.Precision.HIGHEST
    gram_re = jnp.einsum("kfp,lfp->fkl", weighted_re, real_part, precision=high) + jnp.einsum(
        "kfp,lfp->fkl", weighted_im, imag_part, precision=high
    )
    gram_im = jnp.einsum("kfp,lfp->fkl", weighted_re, imag_part, precision=high) - jnp.einsum(
        "kfp,lfp->fkl", weighted_im, real_part, precision=high
    )
    return (gram_re, gram_im)


def stack_entries(entries):
    return jnp.stack([jnp.stack(row_list, axis=1) for row_list in entries], axis=1)


def cholesky_upper(gram_re, gram_im):
    blocks_n = gram_re.shape[-1]
    zeros_f = jnp.zeros_like(gram_re[:, 0, 0])
    fac_re = [[zeros_f for column in range(blocks_n)] for row in range(blocks_n)]
    fac_im = [[zeros_f for column in range(blocks_n)] for row in range(blocks_n)]
    for row in range(blocks_n):
        pivot = gram_re[:, row, row]
        for upper in range(row):
            pivot = (
                pivot
                - fac_re[upper][row] * fac_re[upper][row]
                - fac_im[upper][row] * fac_im[upper][row]
            )
        diagonal = jnp.sqrt(pivot)
        fac_re[row][row] = diagonal
        for column in range(row + 1, blocks_n):
            sum_re = gram_re[:, row, column]
            sum_im = gram_im[:, row, column]
            for upper in range(row):
                sum_re = sum_re - (
                    fac_re[upper][row] * fac_re[upper][column]
                    + fac_im[upper][row] * fac_im[upper][column]
                )
                sum_im = sum_im - (
                    fac_re[upper][row] * fac_im[upper][column]
                    - fac_im[upper][row] * fac_re[upper][column]
                )
            fac_re[row][column] = sum_re / diagonal
            fac_im[row][column] = sum_im / diagonal
    return (stack_entries(fac_re), stack_entries(fac_im))


def invert_upper(fac_re, fac_im):
    blocks_n = fac_re.shape[-1]
    zeros_f = jnp.zeros_like(fac_re[:, 0, 0])
    inv_re = [[zeros_f for column in range(blocks_n)] for row in range(blocks_n)]
    inv_im = [[zeros_f for column in range(blocks_n)] for row in range(blocks_n)]
    for column in range(blocks_n):
        inv_re[column][column] = 1.0 / fac_re[:, column, column]
        for row in range(column - 1, -1, -1):
            sum_re = zeros_f
            sum_im = zeros_f
            for middle in range(row + 1, column + 1):
                sum_re = (
                    sum_re
                    + fac_re[:, row, middle] * inv_re[middle][column]
                    - fac_im[:, row, middle] * inv_im[middle][column]
                )
                sum_im = (
                    sum_im
                    + fac_re[:, row, middle] * inv_im[middle][column]
                    + fac_im[:, row, middle] * inv_re[middle][column]
                )
            pivot = fac_re[:, row, row]
            inv_re[row][column] = -sum_re / pivot
            inv_im[row][column] = -sum_im / pivot
    return (stack_entries(inv_re), stack_entries(inv_im))


def modes_from(realized, inv_re, inv_im, live_mask):
    half_f = realized.shape[1] // 2
    real_part = realized[:, :half_f]
    imag_part = realized[:, half_f:]
    high = lax.Precision.HIGHEST
    basis_re = jnp.einsum("kfp,fkl->lfp", real_part, inv_re, precision=high) - jnp.einsum(
        "kfp,fkl->lfp", imag_part, inv_im, precision=high
    )
    basis_im = jnp.einsum("kfp,fkl->lfp", real_part, inv_im, precision=high) + jnp.einsum(
        "kfp,fkl->lfp", imag_part, inv_re, precision=high
    )
    return jnp.stack([basis_re * live_mask, basis_im * live_mask], axis=0).astype(jnp.bfloat16)


def stack_factors(first, second):
    stack_re = jnp.concatenate([first[0], second[0]], axis=1)
    stack_im = jnp.concatenate([first[1], second[1]], axis=1)
    blocks_n = first[0].shape[-1]
    column_ids = jnp.arange(blocks_n, dtype=jnp.int32)[None, :]
    rows_re = []
    rows_im = []
    for column in range(blocks_n):
        vector_re = stack_re[:, :, column]
        vector_im = stack_im[:, :, column]
        length = jnp.sqrt(jnp.sum(vector_re * vector_re + vector_im * vector_im, axis=1))
        unit_re = (vector_re / length[:, None])[:, :, None]
        unit_im = (vector_im / length[:, None])[:, :, None]
        coef_re = jnp.sum(unit_re * stack_re + unit_im * stack_im, axis=1)
        coef_im = jnp.sum(unit_re * stack_im - unit_im * stack_re, axis=1)
        later = column_ids > column
        coef_re = jnp.where(later, coef_re, 0.0)
        coef_im = jnp.where(later, coef_im, 0.0)
        rows_re.append(jnp.where(column_ids == column, length[:, None], coef_re))
        rows_im.append(coef_im)
        stack_re = stack_re - (unit_re * coef_re[:, None, :] - unit_im * coef_im[:, None, :])
        stack_im = stack_im - (unit_re * coef_im[:, None, :] + unit_im * coef_re[:, None, :])
    return (jnp.stack(rows_re, axis=1), jnp.stack(rows_im, axis=1), first[2] + second[2])


def per_device(snapshots, weights, counts, starts):
    dft_table = window_table()
    shard_count = lax.axis_size("space")
    slab_rows = snapshots.shape[0]
    point_count = snapshots.shape[1] // shard_count
    shaped = snapshots.reshape(slab_rows, shard_count, point_count)
    realized = realize(
        lax.all_to_all(shaped, "space", split_axis=1, concat_axis=0, tiled=True)[:, 0, :],
        starts,
        dft_table,
    )
    live_mask = (jnp.arange(point_count, dtype=jnp.int32) < counts[0]).astype(jnp.float32)
    live_area = weights * live_mask
    gram_re, gram_im = gram_parts(realized, live_area)
    local_area = jnp.sum(live_area)
    local_re, local_im = cholesky_upper(gram_re, gram_im)
    fac_re, fac_im, area_total = combined_all(
        (local_re, local_im, local_area), "space", stack_factors
    )
    norm_scale = 1.0 / jnp.sqrt(area_total)
    fac_re = fac_re * norm_scale
    fac_im = fac_im * norm_scale
    inv_re, inv_im = invert_upper(fac_re, fac_im)
    modes = modes_from(realized, inv_re, inv_im, live_mask)
    return (modes, jnp.stack([fac_re, fac_im], axis=0))


def solution(mesh):
    in_specs = (P("space", "case"), P(("case", "space")), P(("case", "space")), P())
    out_specs = (P(None, None, None, ("case", "space")), P(None, "case", None, None))
    return jax.shard_map(
        per_device, mesh=mesh, in_specs=in_specs, out_specs=out_specs, check_vma=False
    )
```

profile of v0, /device:TPU:15, one launch (start us, length us, event | category | flops | bytes accessed | tf_op | source)
XLA Modules:
  0.0 440.8 jit_solution(2932954055664864114)
XLA Ops:
  0.6 2.3 copy.12068
  2.9 6.7 %all-to-all-start = ((f32[64,16,256]{2,0,1:T(8,128)}), f32[64,16,256]{2,0,1:T(8,128)S(1)}, u32[]{:S(2)}, u32[]{:S(2)}) async-start(f32[64,16,256]{2,0,1:T(8,128)} %bitcast.1512), calls=%async_computation | async-start | bytes 2097152 | tf_op jit(solution)/shard_map/all_to_all | solution.py:171
  11.5 1.3 dynamic-update-slice
  12.8 38.8 %all-reduce = f32[16]{0:T(128)} all-reduce(f32[16]{0:T(128)S(1)} %dynamic-update-slice), channel_id=1, replica_groups=mesh['case'=2,'space'=16] {'space'}, use_global_device_ids=true, to_apply=%add | all-reduce | flops 16 | bytes 128
  76.9 6.7 %stack.191 = f32[8,258,256]{2,0,1:T(8,128)S(1)} concatenate(f32[1,258,256]{2,0,1:T(1,128)} %stack.183, f32[1,258,256]{2,0,1:T(1,128)} %stack.184, f32[1,258,256]{2,0,1:T(1,128)} %stack.185, f32[1,258,256]{2,0,1:T(1,128)S(1)} %stack.186, f32[1,258,256]{2,0,1:T(1,128)S(1)} %stack.187, f32[1,258,256]{2,0,1:T(1,128)S(1)} %stack.188, f32[1,258,256]{2,0,1:T(1,128)S(1)} %stack.189, ...), dimensions={0} | concatenate | bytes 4227072 | tf_op jit(solution)/shard_map/stack | solution.py:43
  83.6 1.1 fusion.12
  84.7 1.1 fusion.24
  85.8 8.9 %slice_reduce_fusion.37 = (f32[129]{0:T(256)S(1)}, f32[129]{0:T(256)S(1)}, f32[129]{0:T(256)S(1)}, f32[129]{0:T(256)S(1)}, f32[129]{0:T(256)S(1)}, /*index=5*/f3...) fusion(f32[129,8,8]{2,1,0:T(8,128)S(1)} %fusion.24), kind=kLoop, calls=%fused_computation.285 | loop fusion | bytes 18576 | tf_op jit(solution)/shard_map/slice | solution.py:82
  94.7 9.9 %slice_reduce_fusion.1 = (f32[129]{0:T(256)S(1)}, f32[129]{0:T(256)S(1)}, f32[129]{0:T(256)S(1)}, f32[129]{0:T(256)S(1)}, f32[129]{0:T(256)S(1)}, /*index=5*/f32...) fusion(f32[129,8,8]{2,1,0:T(8,128)S(1)} %fusion.24), kind=kLoop, calls=%fused_computation.249 | loop fusion | bytes 19608 | tf_op jit(solution)/shard_map/slice | solution.py:72
  104.6 1.1 fusion.10
  105.7 1.1 fusion.27
  106.8 4.0 slice_reduce_fusion.38
  110.9 10.0 %slice_reduce_fusion = (f32[129]{0:T(256)S(1)}, f32[129]{0:T(256)S(1)}, f32[129]{0:T(256)S(1)}, f32[129]{0:T(256)S(1)}, f32[129]{0:T(256)S(1)}, /*index=5*/f32[1...) fusion(f32[129,8,8]{2,1,0:T(8,128)S(1)} %fusion.27), kind=kLoop, calls=%fused_computation.248 | loop fusion | bytes 19608 | tf_op jit(solution)/shard_map/slice | solution.py:83
  122.4 89.0 %all-gather = f32[2064,8,8]{2,1,0:T(8,128)S(1)} all-gather(f32[129,8,8]{2,1,0:T(8,128)S(1)} %copy.12002), channel_id=2, replica_groups=mesh['case'=2,'space'=16] {'space'}, dimensions={0}, use_global_device_ids=true | all-gather | bytes 561408 | tf_op jit(solution)/shard_map/all_gather | solution.py:11
  211.3 3.5 slice.1024
  214.8 2.1 copy-done
  217.3 97.9 %all-gather.1 = f32[2064,8,8]{2,1,0:T(8,128)S(1)} all-gather(f32[129,8,8]{2,1,0:T(8,128)S(1)} %copy.12003), channel_id=3, replica_groups=mesh['case'=2,'space'=16] {'space'}, dimensions={0}, use_global_device_ids=true | all-gather | bytes 561408 | tf_op jit(solution)/shard_map/all_gather | solution.py:11
  315.3 3.6 slice.1025
  319.2 7.1 %copy.12008 = f32[15,129,8,8]{1,3,2,0:T(8,128)} copy(f32[15,129,8,8]{3,2,1,0:T(8,128)} %bitcast.1568) | data formatting | bytes 990720 | tf_op jit(solution)/shard_map/while | solution.py:14
  326.7 7.1 %copy.12009 = f32[15,129,8,8]{1,3,2,0:T(8,128)} copy(f32[15,129,8,8]{3,2,1,0:T(8,128)} %bitcast.1569) | data formatting | bytes 990720 | tf_op jit(solution)/shard_map/while | solution.py:14
  333.8 98.0 %while.14 = (s32[]{:T(128)}, f32[129,8,8]{0,2,1:T(8,128)S(1)}, f32[129,8,8]{0,2,1:T(8,128)S(1)}, f32[]{:T(128)}, f32[15,129,8,8]{1,3,2,0:T(8,128)}, /*index=5*/f32[15,129,8,8]{1,3,2,0:T(8,128)}, f32[15]{0:T(128)S(1)}, s32[]{:T(128)}) while((s32[]{:T(128)}, f32[129,8,8]{0,2,1:T(8,128)S(1)}, f32[129,8,8]{0,2,1:T(8,128)S(1)}, f32[]{:T(128)}, ...), condition=%wide.region_28.29_spmd, body=%wide.region_3.28_spmd.sunk | while | flops 2172489 | bytes 4603589 | solution.py:14
  335.9 0.9 dynamic-slice_bitcast_fusion.3
  342.5 0.9 dynamic-slice_bitcast_fusion.3
  349.0 0.9 dynamic-slice_bitcast_fusion.3
  362.1 0.9 dynamic-slice_bitcast_fusion.3
  368.6 0.9 dynamic-slice_bitcast_fusion.3
  375.1 0.9 dynamic-slice_bitcast_fusion.3
  434.5 1.0 fusion.37
  435.5 1.0 fusion.35
  436.5 1.1 fusion.23
  437.6 1.1 fusion.22
  439.3 1.1 pad_maximum_fusion.2
  (1318 shorter events, 73.4 us)
Async XLA Ops:
  2.9 7.3 %copy-start.3 = (u32[32]{0:T(128)S(1)}, u32[32]{0:T(128)}, u32[]{:S(2)}) copy-start(u32[32]{0:T(128)} %constant.71) | copy-start | bytes 388
  2.9 7.9 %copy-start.2 = (f32[256]{0:T(256)S(1)}, f32[256]{0:T(256)}, u32[]{:S(2)}) copy-start(f32[256]{0:T(256)} %param.7) | copy-start | bytes 3076
  2.9 48.7 %copy-start.1 = (s32[8]{0:T(128)S(1)}, s32[8]{0:T(128)}, u32[]{:S(2)}) copy-start(s32[8]{0:T(128)} %param.9) | copy-start | bytes 100
  2.9 66.8 %all-to-all-start = ((f32[64,16,256]{2,0,1:T(8,128)}), f32[64,16,256]{2,0,1:T(8,128)S(1)}, u32[]{:S(2)}, u32[]{:S(2)}) async-start(f32[64,16,256]{2,0,1:T(8,128)} %bitcast.1512), calls=%async_computation | async-start | bytes 2097152 | tf_op jit(solution)/shard_map/all_to_all | solution.py:171
  211.3 5.7 %copy-start = (f32[2064,8,8]{2,1,0:T(8,128)}, f32[2064,8,8]{2,1,0:T(8,128)S(1)}, u32[]{:S(2)}) copy-start(f32[2064,8,8]{2,1,0:T(8,128)S(1)} %all-gather) | copy-start | bytes 1585156
  315.3 3.7 slice-start
where the time goes:
time: 448 us; the launch traced here: 441 us
  blocking collectives  226 us (50%)
  local copies, waits for them, and re-layouts  100 us (22%)
  other arithmetic  43.3 us (10%)
  loops' own time  35 us (8%)
  between operations  18.4 us (4%)
  matrix products  11.8 us (3%)
  starting transfers between devices  6.69 us (1%)
    all_gather x2, blocking collectives, combined_all(): pieces = jax.tree.map(lambda part: lax.all_gather(part, axis), value)  187 us
    unnamed x1, blocking collectives  38.8 us
    another operation x1, loops' own time, combined_all(): lax.scan(lambda running, piece: (join(running, piece), None), head, tail)  35 us
    while x4, local copies, waits for them, and re-layouts, combined_all(): lax.scan(lambda running, piece: (join(running, piece), None), head, tail)  14.9 us
    slice x2, local copies, waits for them, and re-layouts, cholesky_upper(): sum_im = gram_im[:, row, column]  14 us
    squeeze x15, local copies, waits for them, and re-layouts, combined_all(): lax.scan(lambda running, piece: (join(running, piece), None), head, tail)  13.3 us
    another operation x9, local copies, waits for them, and re-layouts, realize(): return jnp.stack(outputs, axis=0)  10.2 us
    slice x1, local copies, waits for them, and re-layouts, cholesky_upper(): pivot = gram_re[:, row, row]  9.89 us
  transfers between devices with their start and end apart: 1, of which 0 were waited for; matrix products, arithmetic and copies ran while one was open for 1% of the time, Pallas kernels for 0%

commit v1 on v0

v1 whole, which is shorter than its diff:
```python
import functools

import jax
import jax.numpy as jnp
import numpy as np
from jax import lax
from jax.experimental import pallas as pl
from jax.experimental.pallas import tpu as pltpu
from jax.sharding import PartitionSpec as P

NFFT = 256
NBLK = 8
NFREQ = NFFT // 2 + 1
FROWS = 136
LANES = 128
SLOT = 72


def window_table():
    moment = np.arange(NFFT)
    harmonic = np.arange(NFREQ)
    hann = 0.5 - 0.5 * np.cos(2.0 * np.pi * moment / NFFT)
    scale = 1.0 / np.sqrt(np.sum(hann * hann))
    angle = 2.0 * np.pi * (harmonic[:, None] * moment[None, :] % NFFT) / NFFT
    table = np.zeros((2 * FROWS, NFFT))
    table[:NFREQ] = np.cos(angle) * hann * scale
    table[FROWS : FROWS + NFREQ] = -np.sin(angle) * hann * scale
    table = table.astype(np.float32)
    high = table.astype(jnp.bfloat16)
    low = (table - high.astype(np.float32)).astype(jnp.bfloat16)
    both = np.concatenate([high, low], axis=0)
    return np.stack([np.roll(both, turn, axis=1) for turn in range(8)])


def kernel(
    n,
    starts_ref,
    live_ref,
    snap_ref,
    table_hbm,
    modes_ref,
    factor_ref,
    rec,
    table,
    real,
    gram,
    slots,
    coef,
    own_sem,
    table_sem,
    send_a,
    recv_a,
    send_g,
    recv_g,
):
    me = lax.axis_index("space")
    rows = snap_ref.shape[0]
    points = snap_ref.shape[1] // n
    mesh_type = pl.DeviceIdType.MESH

    def peer(step):
        return lax.rem(me + step, n)

    barrier = pltpu.get_barrier_semaphore()

    def greet(step, carry):
        pl.semaphore_signal(
            barrier, inc=1, device_id={"space": peer(step)}, device_id_type=mesh_type
        )
        return carry

    lax.fori_loop(1, n, greet, 0)
    my_rows = pl.ds(pl.multiple_of(me * rows, 8), rows)

    def columns(shard):
        return pl.ds(pl.multiple_of(shard * points, LANES), points)

    own = pltpu.make_async_copy(snap_ref.at[:, columns(me)], rec.at[my_rows, :], own_sem)
    own.start()
    fetch = pltpu.make_async_copy(table_hbm, table, table_sem)
    fetch.start()
    pl.semaphore_wait(barrier, n - 1)

    def block_copy(step):
        dest = peer(step)
        return pltpu.make_async_remote_copy(
            src_ref=snap_ref.at[:, columns(dest)],
            dst_ref=rec.at[my_rows, :],
            send_sem=send_a.at[step],
            recv_sem=recv_a.at[step],
            device_id={"space": dest},
            device_id_type=mesh_type,
        )

    def gram_copy(step):
        return pltpu.make_async_remote_copy(
            src_ref=slots.at[me],
            dst_ref=slots.at[me],
            send_sem=send_g.at[step],
            recv_sem=recv_g.at[step],
            device_id={"space": peer(step)},
            device_id_type=mesh_type,
        )

    def start_all(make):
        def body(step, carry):
            make(step).start()
            return carry

        lax.fori_loop(1, n, body, 0)

    def wait_all(make, sending):
        def body(step, carry):
            if sending:
                make(step).wait_send()
            else:
                make(step).wait_recv()
            return carry

        lax.fori_loop(1, n, body, 0)

    start_all(block_copy)
    live = live_ref[0:1, :]
    area = live_ref[1:2, :]
    own.wait()
    fetch.wait()
    wait_all(block_copy, False)

    record_rows = rows * n
    rec[record_rows : record_rows + 8, :] = jnp.zeros((8, points), jnp.float32)

    def add_rows(chunk, total):
        return total + rec[pl.ds(pl.multiple_of(chunk * 64, 64), 64), :]

    sums = lax.fori_loop(0, record_rows // 64, add_rows, jnp.zeros((64, points), jnp.float32))
    mean = jnp.sum(sums, axis=0, keepdims=True) * (1.0 / record_rows)

    early = lax.broadcasted_iota(jnp.int32, (8, points), 0)

    def transform(block, carry):
        start = starts_ref[block]
        base = lax.div(start, 8) * 8
        shift = start - base
        wrapped = jnp.where(early < shift, rec[pl.ds(base + NFFT, 8), :], rec[pl.ds(base, 8), :])
        segment = jnp.concatenate([wrapped, rec[pl.ds(base + 8, NFFT - 8), :]], axis=0) - mean
        seg_high = segment.astype(jnp.bfloat16)
        seg_low = (segment - seg_high.astype(jnp.float32)).astype(jnp.bfloat16)
        high = table[shift, 0 : 2 * FROWS, :]
        low = table[shift, 2 * FROWS : 4 * FROWS, :]
        dot = functools.partial(jnp.dot, preferred_element_type=jnp.float32)
        real[block] = dot(high, seg_high) + (dot(high, seg_low) + dot(low, seg_high))
        return carry

    lax.fori_loop(0, NBLK, transform, 0)

    lane = lax.broadcasted_iota(jnp.int32, (8, LANES), 1)

    def gram_tile(tile, carry):
        re_rows = pl.ds(pl.multiple_of(tile * 8, 8), 8)
        im_rows = pl.ds(pl.multiple_of(FROWS + tile * 8, 8), 8)
        packed = jnp.zeros((8, LANES), jnp.float32)
        q_re = [real[k, re_rows, :] for k in range(NBLK)]
        q_im = [real[k, im_rows, :] for k in range(NBLK)]
        for k in range(NBLK):
            w_re = q_re[k] * area
            w_im = q_im[k] * area
            for l in range(k, NBLK):
                entry = jnp.sum(w_re * q_re[l] + w_im * q_im[l], axis=1, keepdims=True)
                packed = jnp.where(lane == k * 8 + l, entry, packed)
                if l > k:
                    entry = jnp.sum(w_re * q_im[l] - w_im * q_re[l], axis=1, keepdims=True)
                    packed = jnp.where(lane == (7 - k) * 8 + l - k - 1, entry, packed)
        gram[re_rows, :] = packed
        return carry

    lax.fori_loop(0, FROWS // 8, gram_tile, 0)
    local_area = jnp.sum(area, axis=1, keepdims=True)
    sub = lax.broadcasted_iota(jnp.int32, (8, LANES), 0)
    slots[me, 0:64, :] = jnp.transpose(gram[0:LANES, :])[0:64, :]
    slots[me, 64:SLOT, :] = jnp.where(sub == 1, local_area, gram[LANES:FROWS, :])
    start_all(gram_copy)
    wait_all(gram_copy, False)

    def add_slot(shard, total):
        return total + slots[shard]

    summed = lax.fori_loop(1, n, add_slot, slots[0])
    tail = summed[64:SLOT, :]
    per_area = 1.0 / tail[1:2, :]
    tail_t = jnp.transpose(jnp.concatenate([tail * per_area] * (LANES // 8), axis=0))
    summed = jnp.concatenate([summed[0:64, :] * per_area, tail_t[0:64, :]], axis=1)

    column = lax.broadcasted_iota(jnp.int32, (NBLK, 2 * LANES), 0)
    valid = lax.broadcasted_iota(jnp.int32, (NBLK, 2 * LANES), 1) < NFREQ
    a_re = []
    a_im = []
    for i in range(NBLK):
        unit = jnp.where(column == i, 1.0, 0.0)
        a_re.append(jnp.where(valid, summed[8 * i : 8 * i + 8, :], unit))
        part = summed[8 * (7 - i) : 8 * (7 - i) + 8, :]
        part = pltpu.roll(part, i + 1, 0) if i < NBLK - 1 else part
        a_im.append(jnp.where(valid & (column > i), part, 0.0))
    r_re = []
    r_im = []
    inv_diag = []
    for i in range(NBLK):
        scale = 1.0 / jnp.sqrt(a_re[i][i : i + 1, :])
        inv_diag.append(scale)
        r_re.append(jnp.where(column >= i, a_re[i] * scale, 0.0))
        r_im.append(jnp.where(column > i, a_im[i] * scale, 0.0))
        for k in range(i + 1, NBLK):
            c_re = r_re[i][k : k + 1, :]
            c_im = r_im[i][k : k + 1, :]
            a_re[k] = a_re[k] - (c_re * r_re[i] + c_im * r_im[i])
            a_im[k] = a_im[k] - (c_re * r_im[i] - c_im * r_re[i])
    x_re = [None] * NBLK
    x_im = [None] * NBLK
    for i in range(NBLK - 1, -1, -1):
        sum_re = jnp.where(column == i, 1.0, 0.0)
        sum_im = jnp.zeros((NBLK, 2 * LANES), jnp.float32)
        for m in range(i + 1, NBLK):
            c_re = r_re[i][m : m + 1, :]
            c_im = r_im[i][m : m + 1, :]
            sum_re = sum_re - (c_re * x_re[m] - c_im * x_im[m])
            sum_im = sum_im - (c_re * x_im[m] + c_im * x_re[m])
        x_re[i] = sum_re * inv_diag[i]
        x_im[i] = sum_im * inv_diag[i]

    def by_frequency(parts_re, parts_im):
        stacked = jnp.concatenate(parts_re + parts_im, axis=0)
        head = jnp.transpose(stacked[:, 0:LANES])
        end = jnp.transpose(stacked[:, LANES : 2 * LANES])
        return head, end[0:8, :]

    head, end = by_frequency(x_re, x_im)
    coef[0:LANES, :] = head
    coef[LANES:FROWS, :] = end
    head, end = by_frequency(r_re, r_im)
    factor_ref[0:LANES, :] = head
    factor_ref[LANES:FROWS, :] = end

    def mode_rows(first, count, store):
        re_rows = pl.ds(first, count)
        im_rows = pl.ds(FROWS + first, count)
        c = coef[re_rows, :]
        for l in range(NBLK):
            out_re = jnp.zeros((count, points), jnp.float32)
            out_im = jnp.zeros((count, points), jnp.float32)
            for k in range(l + 1):
                q_re = real[k, re_rows, :]
                q_im = real[k, im_rows, :]
                c_re = c[:, k * 8 + l : k * 8 + l + 1]
                out_re = out_re + q_re * c_re
                out_im = out_im + q_im * c_re
                if k < l:
                    c_im = c[:, 64 + k * 8 + l : 64 + k * 8 + l + 1]
                    out_re = out_re - q_im * c_im
                    out_im = out_im + q_re * c_im
            store(0, l, (out_re * live).astype(jnp.bfloat16))
            store(1, l, (out_im * live).astype(jnp.bfloat16))

    def mode_tile(tile, carry):
        first = pl.multiple_of(tile * 16, 16)

        def store(part, l, value):
            modes_ref[part, l, pl.ds(first, 16), :] = value

        mode_rows(first, 16, store)
        return carry

    lax.fori_loop(0, LANES // 16, mode_tile, 0)

    def store_tail(part, l, value):
        modes_ref[part, l, LANES:NFREQ, :] = value[0 : NFREQ - LANES, :]

    mode_rows(LANES, 8, store_tail)
    wait_all(block_copy, True)
    wait_all(gram_copy, True)


def per_device(snapshots, weights, counts, starts):
    n = lax.axis_size("space")
    rows, width = snapshots.shape
    points = width // n
    live = (jnp.arange(points, dtype=jnp.int32) < counts[0]).astype(jnp.float32)
    vmem = pl.BlockSpec(memory_space=pltpu.VMEM)
    smem = pl.BlockSpec(memory_space=pltpu.SMEM)
    anywhere = pl.BlockSpec(memory_space=pl.ANY)
    dma = pltpu.SemaphoreType.DMA
    modes, factor = pl.pallas_call(
        functools.partial(kernel, n),
        out_shape=(
            jax.ShapeDtypeStruct((2, NBLK, NFREQ, points), jnp.bfloat16),
            jax.ShapeDtypeStruct((FROWS, LANES), jnp.float32),
        ),
        in_specs=[smem, vmem, anywhere, anywhere],
        out_specs=(vmem, vmem),
        scratch_shapes=[
            pltpu.VMEM((rows * n + 8, points), jnp.float32),
            pltpu.VMEM((8, 4 * FROWS, NFFT), jnp.bfloat16),
            pltpu.VMEM((NBLK, 2 * FROWS, points), jnp.float32),
            pltpu.VMEM((FROWS, LANES), jnp.float32),
            pltpu.VMEM((n, SLOT, LANES), jnp.float32),
            pltpu.VMEM((FROWS, LANES), jnp.float32),
            dma,
            dma,
            dma((n,)),
            dma((n,)),
            dma((n,)),
            dma((n,)),
        ],
        compiler_params=pltpu.CompilerParams(
            collective_id=0, has_side_effects=True, vmem_limit_bytes=40 * 2**20
        ),
    )(starts, jnp.stack([live, weights * live]), snapshots, jnp.asarray(window_table()))
    factor = factor[:NFREQ].reshape(NFREQ, 2, NBLK, NBLK)
    return (modes, jnp.moveaxis(factor, 1, 0))


def solution(mesh):
    in_specs = (P("space", "case"), P(("case", "space")), P(("case", "space")), P())
    out_specs = (P(None, None, None, ("case", "space")), P(None, "case", None, None))
    return jax.shard_map(
        per_device, mesh=mesh, in_specs=in_specs, out_specs=out_specs, check_vma=False
    )
```

time: 448 us -> 56.5 us (0.13)
  the two profiles are of different devices: /device:TPU:15 before, /device:TPU:31 now
where the time goes in v1:
time: 56.5 us; the launch traced here: 56.3 us
  Pallas kernels  48.8 us (86%)
  local copies, waits for them, and re-layouts  5.44 us (10%)
  between operations  1.3 us (2%)
  other arithmetic  0.7 us (1%)
    pallas_call x1, Pallas kernels, per_device(): pl.pallas_call(functools.partial(kernel, n), out_shape=(jax.ShapeDtypeStr...  48.8 us
    unnamed x7, local copies, waits for them, and re-layouts  4.68 us

profile of v1, /device:TPU:31, one launch (start us, length us, event | category | flops | bytes accessed | tf_op | source)
XLA Modules:
  0.0 56.3 jit_solution(3436188278575623701)
XLA Ops:
  1.3 0.7 %compare_select_fusion = f32[256]{0:T(256)S(1)} fusion(f32[256]{0:T(256)} %param.6, s32[]{:T(128)} %bitcast.7), kind=kLoop, calls=%fused_computation.2 | loop fusion | flops 512 | bytes 2052 | tf_op jit(solution)/shard_map/mul | solution.py:315
  2.0 0.0 copy-start
  2.0 1.6 %copy-done = bf16[8,544,256]{2,1,0:T(8,128)(2,1)S(1)} copy-done((bf16[8,544,256]{2,1,0:T(8,128)(2,1)S(1)}, bf16[8,544,256]{2,1,0:T(8,128)(2,1)}, u32[]{:S(2)}) %copy-start) | copy-done | bytes 2228248
  3.6 0.0 copy-start.1
  3.6 1.2 %copy-done.1 = f32[64,4096]{1,0:T(8,128)S(1)} copy-done((f32[64,4096]{1,0:T(8,128)S(1)}, f32[64,4096]{1,0:T(8,128)}, u32[]{:S(2)}) %copy-start.1) | copy-done | bytes 1048600
  4.8 0.0 copy-start.2
  4.8 0.7 %copy-done.2 = s32[8]{0:T(128)S(1)} copy-done((s32[8]{0:T(128)S(1)}, s32[8]{0:T(128)}, u32[]{:S(2)}) %copy-start.2) | copy-done | bytes 56
  5.5 48.8 %shard_map.68 = (bf16[2,8,129,256]{3,2,1,0:T(8,128)(2,1)S(1)}, f32[136,128]{1,0:T(8,128)S(1)}) custom-call(s32[8]{0:T(128)S(1)} %copy-done.2, f32[2,256]{1,0:T(2,128)S(1)} %pad_maximum_fusion.live_ref, f32[64,4096]{1,0:T(8,128)S(1)} %copy-done.1, bf16[8,544,256]{2,1,0:T(8,128)(2,1)S(1)} %copy-done), custom_call_target="tpu_custom_call" | custom-call | tf_op jit(solution)/shard_map/pallas_call | solution.py:290
  54.3 1.2 %copy.10 = bf16[2,8,129,256]{3,1,2,0:T(8,128)(2,1)} copy(bf16[2,8,129,256]{3,2,1,0:T(8,128)(2,1)S(1)} %get-tuple-element.8) | data formatting | bytes 2113536
  55.5 0.8 %copy.9 = f32[129,128]{0,1:T(8,128)} copy(f32[129,128]{1,0:T(8,128)S(1)} %bitcast.8) | data formatting | bytes 132096 | tf_op jit(solution)/shard_map/slice | solution.py:316
  (2 shorter events, 0.0 us)
Async XLA Ops:
  2.0 1.6 %copy-start = (bf16[8,544,256]{2,1,0:T(8,128)(2,1)S(1)}, bf16[8,544,256]{2,1,0:T(8,128)(2,1)}, u32[]{:S(2)}) copy-start(bf16[8,544,256]{2,1,0:T(8,128)(2,1)} %constant.4.clone.table_hbm) | copy-start | bytes 6684676
  3.6 1.2 %copy-start.1 = (f32[64,4096]{1,0:T(8,128)S(1)}, f32[64,4096]{1,0:T(8,128)}, u32[]{:S(2)}) copy-start(f32[64,4096]{1,0:T(8,128)} %snap_ref.1) | copy-start | bytes 3145732
  4.8 0.7 %copy-start.2 = (s32[8]{0:T(128)S(1)}, s32[8]{0:T(128)}, u32[]{:S(2)}) copy-start(s32[8]{0:T(128)} %starts_ref.1) | copy-start | bytes 100

commit v2 on v1

--- a/solution.py
+++ b/solution.py
@@ -32,10 +32,15 @@
     return np.stack([np.roll(both, turn, axis=1) for turn in range(8)])
 
 
+def stages_of(n):
+    return [(1, 2), (2, 2), (4, n // 4)]
+
+
 def kernel(
     n,
     starts_ref,
-    live_ref,
+    counts_ref,
+    weights_ref,
     snap_ref,
     table_hbm,
     modes_ref,
@@ -46,94 +51,86 @@
     gram,
     slots,
     coef,
+    send_sem,
+    recv_sem,
     own_sem,
     table_sem,
-    send_a,
-    recv_a,
-    send_g,
-    recv_g,
+    block_send,
+    block_recv,
 ):
     me = lax.axis_index("space")
     rows = snap_ref.shape[0]
     points = snap_ref.shape[1] // n
+    record_rows = rows * n
     mesh_type = pl.DeviceIdType.MESH
 
-    def peer(step):
-        return lax.rem(me + step, n)
+    def peer(stride, size, step):
+        place = lax.rem(lax.div(me, stride), size)
+        return me + (lax.rem(place + step, size) - place) * stride
 
     barrier = pltpu.get_barrier_semaphore()
 
     def greet(step, carry):
         pl.semaphore_signal(
-            barrier, inc=1, device_id={"space": peer(step)}, device_id_type=mesh_type
+            barrier,
+            inc=1,
+            device_id={"space": lax.rem(me + step, n)},
+            device_id_type=mesh_type,
         )
         return carry
 
     lax.fori_loop(1, n, greet, 0)
-    my_rows = pl.ds(pl.multiple_of(me * rows, 8), rows)
+
+    def rows_of(shard):
+        return pl.ds(pl.multiple_of(shard * rows, 8), rows)
 
     def columns(shard):
         return pl.ds(pl.multiple_of(shard * points, LANES), points)
 
-    own = pltpu.make_async_copy(snap_ref.at[:, columns(me)], rec.at[my_rows, :], own_sem)
-    own.start()
-    fetch = pltpu.make_async_copy(table_hbm, table, table_sem)
-    fetch.start()
-    pl.semaphore_wait(barrier, n - 1)
-
-    def block_copy(step):
-        dest = peer(step)
+    def block_copy(turn):
+        step = 1 + lax.rem(turn + n // 2 - 1, n - 1)
+        dest = lax.rem(me + step, n)
         return pltpu.make_async_remote_copy(
             src_ref=snap_ref.at[:, columns(dest)],
-            dst_ref=rec.at[my_rows, :],
-            send_sem=send_a.at[step],
-            recv_sem=recv_a.at[step],
+            dst_ref=rec.at[rows_of(me), :],
+            send_sem=block_send.at[step],
+            recv_sem=block_recv.at[step],
             device_id={"space": dest},
             device_id_type=mesh_type,
         )
 
-    def gram_copy(step):
-        return pltpu.make_async_remote_copy(
-            src_ref=slots.at[me],
-            dst_ref=slots.at[me],
-            send_sem=send_g.at[step],
-            recv_sem=recv_g.at[step],
-            device_id={"space": peer(step)},
+    own = pltpu.make_async_copy(snap_ref.at[:, columns(me)], rec.at[rows_of(me), :], own_sem)
+    fetch = pltpu.make_async_copy(table_hbm, table, table_sem)
+    pl.semaphore_wait(barrier, n - 1)
+
+    def send_block(turn, carry):
+        block_copy(turn).start()
+        return carry
+
+    lax.fori_loop(0, n - 1, send_block, 0)
+    own.start()
+    fetch.start()
+    live = (lax.broadcasted_iota(jnp.int32, (1, points), 1) < counts_ref[0]).astype(jnp.float32)
+    area = weights_ref[...] * live
+
+    own.wait()
+
+    def take_block(turn, total):
+        step = 1 + turn
+        pltpu.make_async_remote_copy(
+            src_ref=snap_ref.at[:, columns(me)],
+            dst_ref=rec.at[rows_of(me), :],
+            send_sem=block_send.at[step],
+            recv_sem=block_recv.at[step],
+            device_id={"space": lax.rem(me + step, n)},
             device_id_type=mesh_type,
-        )
-
-    def start_all(make):
-        def body(step, carry):
-            make(step).start()
-            return carry
-
-        lax.fori_loop(1, n, body, 0)
-
-    def wait_all(make, sending):
-        def body(step, carry):
-            if sending:
-                make(step).wait_send()
-            else:
-                make(step).wait_recv()
-            return carry
-
-        lax.fori_loop(1, n, body, 0)
-
-    start_all(block_copy)
-    live = live_ref[0:1, :]
-    area = live_ref[1:2, :]
-    own.wait()
+        ).wait_recv()
+        return total + rec[rows_of(lax.rem(me + n - step, n)), :]
+
+    sums = lax.fori_loop(0, n - 1, take_block, rec[rows_of(me), :])
+    mean = jnp.sum(sums, axis=0, keepdims=True) * (1.0 / record_rows)
+    rec[record_rows : record_rows + 8, :] = jnp.zeros((8, points), jnp.float32)
     fetch.wait()
-    wait_all(block_copy, False)
-
-    record_rows = rows * n
-    rec[record_rows : record_rows + 8, :] = jnp.zeros((8, points), jnp.float32)
-
-    def add_rows(chunk, total):
-        return total + rec[pl.ds(pl.multiple_of(chunk * 64, 64), 64), :]
-
-    sums = lax.fori_loop(0, record_rows // 64, add_rows, jnp.zeros((64, points), jnp.float32))
-    mean = jnp.sum(sums, axis=0, keepdims=True) * (1.0 / record_rows)
 
     early = lax.broadcasted_iota(jnp.int32, (8, points), 0)
 
@@ -176,15 +173,34 @@
     lax.fori_loop(0, FROWS // 8, gram_tile, 0)
     local_area = jnp.sum(area, axis=1, keepdims=True)
     sub = lax.broadcasted_iota(jnp.int32, (8, LANES), 0)
-    slots[me, 0:64, :] = jnp.transpose(gram[0:LANES, :])[0:64, :]
-    slots[me, 64:SLOT, :] = jnp.where(sub == 1, local_area, gram[LANES:FROWS, :])
-    start_all(gram_copy)
-    wait_all(gram_copy, False)
-
-    def add_slot(shard, total):
-        return total + slots[shard]
-
-    summed = lax.fori_loop(1, n, add_slot, slots[0])
+    head = jnp.transpose(gram[0:LANES, :])[0:64, :]
+    end = jnp.where(sub == 1, local_area, gram[LANES:FROWS, :])
+    summed = jnp.concatenate([head, end], axis=0)
+    copies = []
+    first = 0
+    for stride, size in stages_of(n):
+        place = first + lax.rem(lax.div(me, stride), size)
+        slots[place] = summed
+        group = [
+            pltpu.make_async_remote_copy(
+                src_ref=slots.at[place],
+                dst_ref=slots.at[place],
+                send_sem=send_sem.at[first + step],
+                recv_sem=recv_sem.at[first + step],
+                device_id={"space": peer(stride, size, step)},
+                device_id_type=mesh_type,
+            )
+            for step in range(1, size)
+        ]
+        for copy in group:
+            copy.start()
+        for copy in group:
+            copy.wait_recv()
+        summed = slots[first]
+        for other in range(1, size):
+            summed = summed + slots[first + other]
+        copies += group
+        first += size
     tail = summed[64:SLOT, :]
     per_area = 1.0 / tail[1:2, :]
     tail_t = jnp.transpose(jnp.concatenate([tail * per_area] * (LANES // 8), axis=0))
@@ -235,9 +251,8 @@
     head, end = by_frequency(x_re, x_im)
     coef[0:LANES, :] = head
     coef[LANES:FROWS, :] = end
-    head, end = by_frequency(r_re, r_im)
-    factor_ref[0:LANES, :] = head
-    factor_ref[LANES:FROWS, :] = end
+    for i, part in enumerate(r_re + r_im):
+        factor_ref[i * NBLK : (i + 1) * NBLK, :] = part[:, 0:NFREQ]
 
     def mode_rows(first, count, store):
         re_rows = pl.ds(first, count)
@@ -274,47 +289,53 @@
         modes_ref[part, l, LANES:NFREQ, :] = value[0 : NFREQ - LANES, :]
 
     mode_rows(LANES, 8, store_tail)
-    wait_all(block_copy, True)
-    wait_all(gram_copy, True)
+    for copy in copies:
+        copy.wait_send()
+
+    def sent_block(turn, carry):
+        block_copy(turn).wait_send()
+        return carry
+
+    lax.fori_loop(0, n - 1, sent_block, 0)
 
 
 def per_device(snapshots, weights, counts, starts):
     n = lax.axis_size("space")
     rows, width = snapshots.shape
     points = width // n
-    live = (jnp.arange(points, dtype=jnp.int32) < counts[0]).astype(jnp.float32)
     vmem = pl.BlockSpec(memory_space=pltpu.VMEM)
     smem = pl.BlockSpec(memory_space=pltpu.SMEM)
+    slot_count = sum(size for stride, size in stages_of(n))
     anywhere = pl.BlockSpec(memory_space=pl.ANY)
     dma = pltpu.SemaphoreType.DMA
     modes, factor = pl.pallas_call(
         functools.partial(kernel, n),
         out_shape=(
             jax.ShapeDtypeStruct((2, NBLK, NFREQ, points), jnp.bfloat16),
-            jax.ShapeDtypeStruct((FROWS, LANES), jnp.float32),
+            jax.ShapeDtypeStruct((2 * NBLK * NBLK, NFREQ), jnp.float32),
         ),
-        in_specs=[smem, vmem, anywhere, anywhere],
+        in_specs=[smem, smem, vmem, anywhere, anywhere],
         out_specs=(vmem, vmem),
         scratch_shapes=[
             pltpu.VMEM((rows * n + 8, points), jnp.float32),
             pltpu.VMEM((8, 4 * FROWS, NFFT), jnp.bfloat16),
             pltpu.VMEM((NBLK, 2 * FROWS, points), jnp.float32),
             pltpu.VMEM((FROWS, LANES), jnp.float32),
-            pltpu.VMEM((n, SLOT, LANES), jnp.float32),
+            pltpu.VMEM((slot_count, SLOT, LANES), jnp.float32),
             pltpu.VMEM((FROWS, LANES), jnp.float32),
+            dma((slot_count,)),
+            dma((slot_count,)),
             dma,
             dma,
             dma((n,)),
             dma((n,)),
-            dma((n,)),
-            dma((n,)),
         ],
         compiler_params=pltpu.CompilerParams(
-            collective_id=0, has_side_effects=True, vmem_limit_bytes=40 * 2**20
+            collective_id=0, has_side_effects=True, vmem_limit_bytes=60 * 2**20
         ),
-    )(starts, jnp.stack([live, weights * live]), snapshots, jnp.asarray(window_table()))
-    factor = factor[:NFREQ].reshape(NFREQ, 2, NBLK, NBLK)
-    return (modes, jnp.moveaxis(factor, 1, 0))
+    )(starts, counts, weights[None, :], snapshots, jnp.asarray(window_table()))
+    factor = factor.reshape(2, NBLK, NBLK, NFREQ)
+    return (modes, jnp.moveaxis(factor, 3, 1))
 
 
 def solution(mesh):

time: 56.5 us -> 53.2 us (0.942)
  the two profiles are of different devices: /device:TPU:31 before, /device:TPU:0 now
where the time goes in v2:
time: 53.2 us; the launch traced here: 53 us
  Pallas kernels  48.6 us (91%)
  local copies, waits for them, and re-layouts  3.12 us (6%)
  between operations  1.29 us (2%)
    pallas_call x1, Pallas kernels, per_device(): pl.pallas_call(functools.partial(kernel, n), out_shape=(jax.ShapeDtypeStr...  48.6 us
    unnamed x4, local copies, waits for them, and re-layouts  3.12 us

profile of v2, /device:TPU:0, one launch (start us, length us, event | category | flops | bytes accessed | tf_op | source)
XLA Modules:
  0.0 53.0 jit_solution(5231235154261499563)
XLA Ops:
  1.3 48.6 %shard_map.68 = (bf16[2,8,129,256]{3,2,1,0:T(8,128)(2,1)}, f32[128,129]{1,0:T(8,128)}) custom-call(s32[8]{0:T(128)} %starts_ref.1, s32[1]{0:T(128)S(6)} %copy.9.counts_ref, f32[1,256]{1,0:T(1,128)} %bitcast.5, f32[64,4096]{1,0:T(8,128)} %snap_ref.1, bf16[8,544,256]{2,1,0:T(8,128)(2,1)} %constant.2.clone.table_hbm), custom_call_target="tpu_custom_call" | custom-call | tf_op jit(solution)/shard_map/pallas_call | solution.py:311
  49.9 0.0 copy-start
  49.9 2.5 %copy.7 = bf16[2,8,129,256]{3,1,2,0:T(8,128)(2,1)} copy(bf16[2,8,129,256]{3,2,1,0:T(8,128)(2,1)} %get-tuple-element.6) | data formatting | bytes 2113536
  52.4 0.0 copy-done
  52.4 0.7 %copy.10 = f32[2,129,8,8]{1,3,2,0:T(8,128)} copy(f32[2,129,8,8]{1,3,2,0:T(8,128)S(1)} %bitcast.4) | data formatting | bytes 132096
Async XLA Ops:
  49.9 2.5 %copy-start = (f32[128,129]{1,0:T(8,128)S(1)}, f32[128,129]{1,0:T(8,128)}, u32[]{:S(2)}) copy-start(f32[128,129]{1,0:T(8,128)} %get-tuple-element.5) | copy-start | bytes 198148

commit v3 on v2

--- a/solution.py
+++ b/solution.py
@@ -148,7 +148,7 @@
         real[block] = dot(high, seg_high) + (dot(high, seg_low) + dot(low, seg_high))
         return carry
 
-    lax.fori_loop(0, NBLK, transform, 0)
+    lax.fori_loop(0, NBLK, transform, 0, unroll=4)
 
     lane = lax.broadcasted_iota(jnp.int32, (8, LANES), 1)
 

time: 53.2 us -> 52.2 us (0.981)
  Pallas kernels: 48.6 us -> 47.6 us
    pallas_call x1, Pallas kernels: 48.6 us -> 47.6 us  [per_device(): pl.pallas_call(functools.partial(kernel, n), out_shape=(jax.ShapeDtypeStr...]
where the time goes in v3:
time: 52.2 us; the launch traced here: 52 us
  Pallas kernels  47.6 us (91%)
  local copies, waits for them, and re-layouts  3.12 us (6%)
  between operations  1.29 us (2%)
    pallas_call x1, Pallas kernels, per_device(): pl.pallas_call(functools.partial(kernel, n), out_shape=(jax.ShapeDtypeStr...  47.6 us
    unnamed x4, local copies, waits for them, and re-layouts  3.12 us

profile of v3, /device:TPU:0, one launch (start us, length us, event | category | flops | bytes accessed | tf_op | source)
XLA Modules:
  0.0 52.0 jit_solution(91029542255911828)
XLA Ops:
  1.3 47.6 %shard_map.68 = (bf16[2,8,129,256]{3,2,1,0:T(8,128)(2,1)}, f32[128,129]{1,0:T(8,128)}) custom-call(s32[8]{0:T(128)} %starts_ref.1, s32[1]{0:T(128)S(6)} %copy.9.counts_ref, f32[1,256]{1,0:T(1,128)} %bitcast.5, f32[64,4096]{1,0:T(8,128)} %snap_ref.1, bf16[8,544,256]{2,1,0:T(8,128)(2,1)} %constant.2.clone.table_hbm), custom_call_target="tpu_custom_call" | custom-call | tf_op jit(solution)/shard_map/pallas_call | solution.py:311
  48.9 0.0 copy-start
  48.9 2.5 %copy.7 = bf16[2,8,129,256]{3,1,2,0:T(8,128)(2,1)} copy(bf16[2,8,129,256]{3,2,1,0:T(8,128)(2,1)} %get-tuple-element.6) | data formatting | bytes 2113536
  51.4 0.0 copy-done
  51.4 0.7 %copy.10 = f32[2,129,8,8]{1,3,2,0:T(8,128)} copy(f32[2,129,8,8]{1,3,2,0:T(8,128)S(1)} %bitcast.4) | data formatting | bytes 132096
Async XLA Ops:
  48.9 2.5 %copy-start = (f32[128,129]{1,0:T(8,128)S(1)}, f32[128,129]{1,0:T(8,128)}, u32[]{:S(2)}) copy-start(f32[128,129]{1,0:T(8,128)} %get-tuple-element.5) | copy-start | bytes 198148
